TPU v7x, 32 devices: a whole 2x2x4 slice. The times are simulated.
32 devices in a mesh: space: 16 (over z, y, core), snap: 2 (over x).
Axes of the slice: x: 2, y: 2, z: 4, core: 2. Of those that a mesh axis runs over, the one named last changes fastest.
Arguments:
- snaps_primal: bfloat16 [512, 49152], P('snap', 'space'), may hold values from -6 to 6
- snaps_adjoint: bfloat16 [512, 49152], P('snap', 'space'), may hold values from -6 to 6
- coef_primal: bfloat16 [512, 256], P('snap'), may hold values from -0.375 to 0.375
- coef_adjoint: bfloat16 [512, 256], P('snap'), may hold values from -0.375 to 0.375
- op_blocks: bfloat16 [384, 5, 128, 128], P('space'), may hold values from -0.25 to 0.25
- counts: int32 [384], P('space'), may hold values from 1 to 5, as said below
- col_index: int32 [384, 5], P('space'), may hold values from 0 to 47, as said below
- ghost_send: int32 [16, 4, 6], P('space'), may hold values from 0 to 23, as said below
Outputs:
- primal_modes: bfloat16 [256, 49152], P('snap', 'space')
- applied: bfloat16 [256, 49152], P('snap', 'space')
- reduced_operator: float32 [256, 256], P(None, 'snap')
- cross_gram: float32 [256, 256], P(None, 'snap')
Inputs may be any that keep to these rules, and one draw needn't show every extreme that they name: `counts`: every block row has its slot 0 live. `col_index`: slot 0 of every block row names the row's own diagonal block; ghost entries never name a partition outside 0 to 15. `ghost_send`: the 6 entries of one list are distinct.
All inputs are finite; a program needn't handle non-finite values.
Results may differ from a plain program's by a relative error of at most 0.02.
Values may be sent and summed in bfloat16 or wider, within the bound.
A program may use at most 64 MiB of HBM per device.

v0:
```python
import math

import jax
import jax.numpy as jnp
from jax import lax
from jax.sharding import PartitionSpec as P


def passed_along(value, axis, steps):
    count = lax.axis_size(axis)
    first, last = (max(0, -steps), min(count, count - steps))
    return lax.ppermute(value, axis, [(source, source + steps) for source in range(first, last)])


def project(coef, snaps):
    return jnp.einsum("mr,ms->rs", coef, snaps, preferred_element_type=jnp.float32)


def per_device(
    snaps_primal, snaps_adjoint, coef_primal, coef_adjoint, op_blocks, counts, col_index, ghost_send
):
    share = coef_primal.shape[1] // lax.axis_size("snap")
    unknowns = snaps_primal.shape[1]
    row_count = col_index.shape[0]
    slot_count = col_index.shape[1]
    block_size = op_blocks.shape[2]
    list_len = ghost_send.shape[2]
    both_shares = lax.psum_scatter(
        jnp.concatenate(
            [project(coef_primal, snaps_primal), project(coef_adjoint, snaps_adjoint)], axis=1
        ).astype(jnp.bfloat16),
        "snap",
        scatter_dimension=0,
        tiled=True,
    )
    primal_share = both_shares[:, :unknowns]
    adjoint_share = both_shares[:, unknowns:]
    blocks = primal_share.reshape(share, row_count, block_size)
    outgoing = jnp.take(blocks, ghost_send[0], axis=1)
    from_far_low = passed_along(outgoing[:, 0], "space", 2)
    from_near_low = passed_along(outgoing[:, 1], "space", 1)
    from_near_high = passed_along(outgoing[:, 2], "space", -1)
    from_far_high = passed_along(outgoing[:, 3], "space", -2)
    received = jnp.stack([from_far_low, from_near_low, from_near_high, from_far_high], axis=1)
    extended = jnp.concatenate([blocks, received.reshape(share, 4 * list_len, block_size)], axis=1)
    picked = jnp.take(extended, col_index, axis=1)
    live = (jnp.arange(slot_count, dtype=jnp.int32)[None, :] < counts[:, None]).astype(jnp.bfloat16)
    picked = picked * live[None, :, :, None]
    applied = jnp.einsum("mrkc,rkjc->mrj", picked, op_blocks, preferred_element_type=jnp.float32)
    applied = applied.astype(jnp.bfloat16).reshape(share, unknowns)
    stacked = jnp.concatenate([applied, primal_share], axis=0)
    products = jnp.einsum(
        "as,bs->ab",
        lax.all_gather(adjoint_share, "snap", axis=0, tiled=True),
        stacked,
        preferred_element_type=jnp.float32,
    )
    factor = 1.0 / math.sqrt(unknowns * lax.axis_size("space"))
    reduced, gram = lax.psum((products[:, :share], products[:, share:]), "space")
    return (primal_share, applied, reduced * factor, gram * factor)


def solution(mesh):
    placed = (
        P("snap", "space"),
        P("snap", "space"),
        P("snap", None),
        P("snap", None),
        P("space", None, None, None),
        P("space"),
        P("space", None),
        P("space", None, None),
    )
    return jax.shard_map(
        per_device,
        mesh=mesh,
        in_specs=placed,
        out_specs=(P("snap", "space"), P("snap", "space"), P(None, "snap"), P(None, "snap")),
        check_vma=False,
    )
```

profile of v0, /device:TPU:3, one launch (start us, length us, event | category | flops | bytes accessed | tf_op | source)
XLA Modules:
  0.0 190.5 jit_solution(15660911934500298614)
XLA Ops:
  7.2 1.3 copy-done
  8.6 1.5 convolution_convert_fusion
  10.1 0.6 convolution_convert_fusion.1
  10.7 1.9 pad_maximum_fusion
  12.7 0.6 copy-done.9
  13.7 42.6 %reduce-scatter.2.cloned.1.call-done = bf16[128,6144]{1,0:T(8,128)(2,1)} async-done(((bf16[256,6144]{1,0:T(8,128)(2,1)}), bf16[128,6144]{1,0:T(8,128)(2,1)}) %reduce-scatter.2.cloned.1.call-update) | async-done | bytes 1572880 | tf_op jit(solution)/shard_map/reduce_scatter | solution.py:28
  56.4 2.4 %fusion.16 = (bf16[128,3072]{1,0:T(8,128)(2,1)}, bf16[128,3072]{1,0:T(8,128)(2,1)S(1)}) fusion(bf16[128,6144]{1,0:T(8,128)(2,1)} %reduce-scatter.2.cloned.1.call-done), kind=kLoop, calls=%fused_computation.38 | loop fusion | bytes 3145728 | tf_op jit(solution)/shard_map/slice | solution.py:37
  58.7 0.9 copy-done.3
  59.6 0.2 copy_bitcast_fusion
  59.9 0.7 gather_fusion
  60.8 1.4 collective-permute-start.3
  62.3 4.0 %collective-permute-start = (bf16[128,6,128]{2,0,1:T(8,128)(2,1)S(1)}, bf16[128,6,128]{2,0,1:T(8,128)(2,1)S(1)}, u32[]{:S(2)}, u32[]{:S(2)}) collective-permute-start(bf16[128,6,128]{2,0,1:T(8,128)(2,1)S(1)} %get-tuple-element.8), channel_id=1, source_target_pairs={{0,4},{2,6},{4,8},{6,10},{8,12},{10,14},{12,16},{14,18},{16,20},{1... | collective-permute-start | bytes 589832 | tf_op jit(solution)/shard_map/ppermute | solution.py:12
  66.3 5.2 %collective-permute-start.1 = (bf16[128,6,128]{2,0,1:T(8,128)(2,1)S(1)}, bf16[128,6,128]{2,0,1:T(8,128)(2,1)S(1)}, u32[]{:S(2)}, u32[]{:S(2)}) collective-permute-start(bf16[128,6,128]{2,0,1:T(8,128)(2,1)S(1)} %get-tuple-element.11), channel_id=1, source_target_pairs={{0,2},{2,4},{4,6},{6,8},{8,10},{10,12},{12,14},{14,16},{16,18},{18... | collective-permute-start | bytes 589832 | tf_op jit(solution)/shard_map/ppermute | solution.py:12
  71.5 1.9 %collective-permute-start.2 = (bf16[128,6,128]{2,0,1:T(8,128)(2,1)S(1)}, bf16[128,6,128]{2,0,1:T(8,128)(2,1)S(1)}, u32[]{:S(2)}, u32[]{:S(2)}) collective-permute-start(bf16[128,6,128]{2,0,1:T(8,128)(2,1)S(1)} %get-tuple-element.10), channel_id=1, source_target_pairs={{2,0},{4,2},{6,4},{8,6},{10,8},{12,10},{14,12},{16,14},{18,16},{20... | collective-permute-start | bytes 589832 | tf_op jit(solution)/shard_map/ppermute | solution.py:12
  73.5 0.4 collective-permute-done
  73.9 4.3 %collective-permute-done.1 = bf16[128,6,128]{2,0,1:T(8,128)(2,1)S(1)} collective-permute-done((bf16[128,6,128]{2,0,1:T(8,128)(2,1)S(1)}, bf16[128,6,128]{2,0,1:T(8,128)(2,1)S(1)}, u32[]{:S(2)}, u32[]{:S(2)}) %collective-permute-start.1) | collective-permute-done | bytes 196640 | tf_op jit(solution)/shard_map/ppermute | solution.py:12
  78.2 0.7 collective-permute-done.2
  79.1 2.9 %gather_fusion.1 = bf16[120,128,128]{2,1,0:T(8,128)(2,1)} fusion(bf16[128,48,128]{2,0,1:T(8,128)(2,1)S(1)} %pad_maximum_fusion.1, s32[1024]{0:T(1024)S(1)} %pad_clamp_fusion), kind=kCustom, calls=%fused_computation.1 | custom fusion | bytes 7864800 | tf_op jit(solution)/shard_map/jit(_take)/gather | solution.py:46
  82.1 5.7 %bitcast_convert_fusion = bf16[24,128,128]{1,2,0:T(8,128)(2,1)} fusion(bf16[24,5,128,128]{3,2,1,0:T(8,128)(2,1)} %param.12, bf16[24,5,128,128]{3,2,1,0:T(8,128)(2,1)} %bitcast.47, pred[24,5]{1,0:T(8,128)(4,1)S(1)} %copy.20, bf16[24,5]{1,0:T(8,128)(2,1)S(1)} %fusion.13), kind=kOutput, calls=%fused_computation.17 | convolution fusion | flops 507641856 | bytes 8651112 | tf_op jit(solution)/shard_map/mrkc,rkjc->mrj/dot_general | solution.py:49
  87.8 1.5 copy.26
  89.3 2.3 %fusion.7 = f32[256,256]{1,0:T(8,128)S(1)} fusion(bf16[256,3072]{1,0:T(8,128)(2,1)} %all-gather.2.cloned.1.call-done, bf16[128,3072]{1,0:T(8,128)(2,1)S(1)} %copy-done.4, bf16[128,3072]{1,0:T(8,128)(2,1)S(1)} %copy.26), kind=kOutput, calls=%fused_computation.13 | convolution fusion | flops 405798912 | bytes 3407872 | tf_op jit(solution)/shard_map/as,bs->ab/dot_general | solution.py:52
  91.6 0.7 fusion.17
  92.4 90.0 %all-reduce.3.cloned.1.call-done = (f32[256,128]{1,0:T(8,128)}, f32[256,128]{1,0:T(8,128)}) async-done(((f32[256,128]{1,0:T(8,128)}, f32[256,128]{1,0:T(8,128)}), (f32[256,128]{1,0:T(8,128)}, f32[256,128]{1,0:T(8,128)})) %all-reduce.3.cloned.1.call-update) | async-done | bytes 262160 | tf_op jit(solution)/shard_map/psum | solution.py:59
  182.3 1.7 broadcast_multiply_fusion
  (42 shorter events, 1.2 us)
Async XLA Ops:
  7.2 1.4 copy-start
  7.2 2.9 %copy-start.7 = (bf16[256,256]{1,0:T(8,128)(2,1)S(1)}, bf16[256,256]{1,0:T(8,128)(2,1)}, u32[]{:S(2)}) copy-start(bf16[256,256]{1,0:T(8,128)(2,1)} %param.10) | copy-start | bytes 393220
  7.2 2.9 %copy-start.5 = (bf16[256,3072]{1,0:T(8,128)(2,1)S(1)}, bf16[256,3072]{1,0:T(8,128)(2,1)}, u32[]{:S(2)}) copy-start(bf16[256,3072]{1,0:T(8,128)(2,1)} %param.8) | copy-start | bytes 4718596
  7.2 49.2 %reduce-scatter.2.cloned.1.call-start = ((), (), s32[]{:S(2)}) async-start(), calls=%async_computation.1 | async-start | bytes 4718592 | tf_op jit(solution)/shard_map/reduce_scatter | solution.py:28
  12.6 0.7 copy-start.9
  12.6 0.8 copy-start.8
  12.6 76.7 %all-gather.2.cloned.1.call-start = ((), (), s32[]{:S(2)}) async-start(), calls=%async_computation.2 | async-start | bytes 2359296 | tf_op jit(solution)/shard_map/all_gather | solution.py:54
  58.7 0.9 copy-start.3
  59.8 1.0 copy-start.1
  59.9 122.5 %all-reduce.3.cloned.1.call-start = ((), (), s32[]{:S(2)}) async-start(), calls=%async_computation.3 | async-start | bytes 524288 | tf_op jit(solution)/shard_map/psum | solution.py:59
  60.6 12.8 %copy-start.10 = (s32[24]{0:T(128)S(1)}, s32[24]{0:T(128)}, u32[]{:S(2)}) copy-start(s32[24]{0:T(128)} %param.13) | copy-start | bytes 292
  60.8 18.1 %copy-start.2 = (bf16[128,24,128]{2,0,1:T(8,128)(2,1)S(1)}, bf16[128,24,128]{2,0,1:T(8,128)(2,1)}, u32[]{:S(2)}) copy-start(bf16[128,24,128]{2,0,1:T(8,128)(2,1)} %copy-done.1) | copy-start | bytes 2359300
  60.8 12.6 %collective-permute-start.3 = (bf16[128,6,128]{2,0,1:T(8,128)(2,1)S(1)}, bf16[128,6,128]{2,0,1:T(8,128)(2,1)S(1)}, u32[]{:S(2)}, u32[]{:S(2)}) collective-permute-start(bf16[128,6,128]{2,0,1:T(8,128)(2,1)S(1)} %get-tuple-element.9), channel_id=1, source_target_pairs={{4,0},{6,2},{8,4},{10,6},{12,8},{14,10},{16,12},{18,14},{20,16},{2... | collective-permute-start | bytes 589832 | tf_op jit(solution)/shard_map/ppermute | solution.py:12
  62.3 11.6 %collective-permute-start = (bf16[128,6,128]{2,0,1:T(8,128)(2,1)S(1)}, bf16[128,6,128]{2,0,1:T(8,128)(2,1)S(1)}, u32[]{:S(2)}, u32[]{:S(2)}) collective-permute-start(bf16[128,6,128]{2,0,1:T(8,128)(2,1)S(1)} %get-tuple-element.8), channel_id=1, source_target_pairs={{0,4},{2,6},{4,8},{6,10},{8,12},{10,14},{12,16},{14,18},{16,20},{1... | collective-permute-start | bytes 589832 | tf_op jit(solution)/shard_map/ppermute | solution.py:12
  66.3 11.9 %collective-permute-start.1 = (bf16[128,6,128]{2,0,1:T(8,128)(2,1)S(1)}, bf16[128,6,128]{2,0,1:T(8,128)(2,1)S(1)}, u32[]{:S(2)}, u32[]{:S(2)}) collective-permute-start(bf16[128,6,128]{2,0,1:T(8,128)(2,1)S(1)} %get-tuple-element.11), channel_id=1, source_target_pairs={{0,2},{2,4},{4,6},{6,8},{8,10},{10,12},{12,14},{14,16},{16,18},{18... | collective-permute-start | bytes 589832 | tf_op jit(solution)/shard_map/ppermute | solution.py:12
  71.5 7.4 %collective-permute-start.2 = (bf16[128,6,128]{2,0,1:T(8,128)(2,1)S(1)}, bf16[128,6,128]{2,0,1:T(8,128)(2,1)S(1)}, u32[]{:S(2)}, u32[]{:S(2)}) collective-permute-start(bf16[128,6,128]{2,0,1:T(8,128)(2,1)S(1)} %get-tuple-element.10), channel_id=1, source_target_pairs={{2,0},{4,2},{6,4},{8,6},{10,8},{12,10},{14,12},{16,14},{18,16},{20... | collective-permute-start | bytes 589832 | tf_op jit(solution)/shard_map/ppermute | solution.py:12
  87.8 1.5 copy-start.4
  89.3 2.3 %copy-start.6 = (bf16[128,3072]{1,0:T(8,128)(2,1)}, bf16[128,3072]{1,0:T(8,128)(2,1)S(1)}, u32[]{:S(2)}) copy-start(bf16[128,3072]{1,0:T(8,128)(2,1)S(1)} %copy.26) | copy-start | bytes 2359300
Sparse Core Ops, SparseCore 0:
  12.7 43.5 reduce-scatter.1
  60.0 27.2 all-gather.1
  92.5 89.8 all-reduce.2
where the time goes:
time: 192 us; the launch traced here: 191 us
  waiting for transfers between devices  138 us (72%)
  between operations  14 us (7%)
  starting transfers between devices  12.7 us (7%)
  local copies, waits for them, and re-layouts  11.7 us (6%)
  matrix products  10.1 us (5%)
  other arithmetic  4.07 us (2%)
    psum x1, waiting for transfers between devices, per_device(): lax.psum((products[:, :share], products[:, share:]), 'space')  90 us
    reduce_scatter x1, waiting for transfers between devices, per_device(): lax.psum_scatter(jnp.concatenate([project(coef_primal, snaps_primal), pro...  42.6 us
    ppermute x4, starting transfers between devices, passed_along(): lax.ppermute(value, axis, [(source, source + steps) for source in range(f...  12.5 us
    dot_general x1, matrix products, per_device(): jnp.einsum('mrkc,rkjc->mrj', picked, op_blocks, preferred_element_type=jn...  5.73 us
    ppermute x4, waiting for transfers between devices, passed_along(): lax.ppermute(value, axis, [(source, source + steps) for source in range(f...  5.38 us
  transfers between devices with their start and end apart: 7, of which 5 were waited for; matrix products, arithmetic and copies ran while one was open for 6% of the time, Pallas kernels for 0%

commit v1 on v0

v1 whole, which is shorter than its diff:
```python
import math

import jax
import jax.numpy as jnp
from jax import lax
from jax.experimental import pallas as pl
from jax.experimental.pallas import tpu as pltpu
from jax.sharding import PartitionSpec as P

MESH = pl.DeviceIdType.MESH
BF16 = jnp.bfloat16
F32 = jnp.float32
OFFSETS = (-2, -1, 1, 2)
TILE_BLOCKS = 4
CHUNK = 64


class Sizes:
    def __init__(self, n_space, n_snap, snaps, coef, op_blocks, ghost_send):
        self.n_space, self.n_snap = n_space, n_snap
        self.devices = n_space * n_snap
        self.snaps, self.unknowns = snaps.shape
        self.modes = coef.shape[1]
        self.share = self.modes // n_snap
        self.rows, self.slots, self.bs = op_blocks.shape[:3]
        self.lists, self.list_len = ghost_send.shape[1:]
        self.mc = CHUNK
        self.chunks = self.modes // self.mc
        self.piece = max(16, self.modes // n_space)
        self.owners = self.modes // self.piece
        self.tiles = self.rows // TILE_BLOCKS
        self.factor = 1.0 / math.sqrt(self.unknowns * n_space)

    def groups(self, c):
        first, last = c * self.mc, (c + 1) * self.mc
        found = []
        for x in range(self.n_snap):
            lo, hi = max(first, x * self.share), min(last, (x + 1) * self.share)
            if lo < hi:
                found.append((x, lo - x * self.share, lo - first, hi - lo))
        return found


def scratch_of(z):
    b, mc, bs = z.rows, z.mc, z.bs
    one = {
        "q": pltpu.VMEM((b, mc, bs), BF16),
        "qr": pltpu.VMEM((z.n_snap - 1, b, mc, bs), BF16),
        "own": pltpu.VMEM((b, mc, bs), BF16),
        "ext": pltpu.VMEM((b + z.lists * z.list_len, mc, bs), BF16),
        "snd": pltpu.VMEM((z.lists, z.list_len, mc, bs), BF16),
        "st": pltpu.VMEM((b, 2 * mc, bs), BF16),
        "d": pltpu.VMEM((z.owners, z.piece, 2 * mc), BF16),
        "rs": pltpu.VMEM((z.devices, z.piece, 2 * mc), BF16),
        "gs": pltpu.VMEM((z.piece, 2 * mc), F32),
        "gat": pltpu.VMEM((z.n_space, z.piece, 2 * mc), F32),
    }
    sem = pltpu.SemaphoreType.DMA
    return {
        "sp": pltpu.VMEM((z.snaps, z.unknowns), BF16),
        "sa": pltpu.VMEM((z.snaps, z.unknowns), BF16),
        "cp": pltpu.VMEM((z.snaps, z.modes), BF16),
        "ca": pltpu.VMEM((z.snaps, z.modes), BF16),
        "op": pltpu.VMEM((z.rows, z.slots, bs, bs), BF16),
        "adj": pltpu.VMEM((z.modes, z.unknowns), BF16),
        "cpt": pltpu.VMEM((z.modes, z.snaps), BF16),
        "load": sem((5,)),
        "q_s": sem((z.chunks, z.n_snap - 1)),
        "q_r": sem((z.chunks, z.n_snap - 1)),
        "g_s": sem((z.chunks, z.lists)),
        "g_r": sem((z.chunks, z.lists)),
        "rs_s": sem((z.chunks,)),
        "rs_r": sem((z.chunks,)),
        "ag_s": sem((z.chunks,)),
        "ag_r": sem((z.chunks,)),
        "chunk": [dict(one) for _ in range(z.chunks)],
    }


def transposed(value):
    return value.astype(F32).T.astype(BF16)


def contract_last(a, b):
    return lax.dot_general(a, b, (((1,), (1,)), ((), ())), preferred_element_type=F32)


def loop(count, body):
    def step(i, carry):
        body(i)
        return carry

    lax.fori_loop(0, count, step, 0)


def kernel(z, sp_hbm, sa_hbm, cp_hbm, ca_hbm, op_hbm, counts, cols, ghosts,
           primal_out, applied_out, reduced_out, gram_out, s):
    space, snap = lax.axis_index("space"), lax.axis_index("snap")
    me = space * z.n_snap + snap
    bs, mc = z.bs, z.mc
    width = TILE_BLOCKS * bs

    loads = [
        pltpu.make_async_copy(source, s[name], s["load"].at[i])
        for i, (source, name) in enumerate(
            [(cp_hbm, "cp"), (sp_hbm, "sp"), (ca_hbm, "ca"), (sa_hbm, "sa"), (op_hbm, "op")]
        )
    ]
    for copy in loads:
        copy.start()

    barrier = pltpu.get_barrier_semaphore()

    def greet(i):
        other = lax.rem(me + 1 + i, z.devices)
        pl.semaphore_signal(
            barrier,
            inc=1,
            device_id=(lax.div(other, z.n_snap), lax.rem(other, z.n_snap)),
            device_id_type=MESH,
        )

    loop(z.devices - 1, greet)

    def columns(t):
        return pl.ds(pl.multiple_of(t * width, width), width)

    def project(c):
        coef = s["cpt"][c * mc:(c + 1) * mc, :]
        q = s["chunk"][c]["q"]

        def tile(t):
            part = jnp.dot(coef, s["sp"][:, columns(t)], preferred_element_type=F32).astype(BF16)
            for i in range(TILE_BLOCKS):
                q[t * TILE_BLOCKS + i] = part[:, i * bs:(i + 1) * bs]

        loop(z.tiles, tile)

    def partial_copy(c, i):
        k = s["chunk"][c]
        return pltpu.make_async_remote_copy(
            src_ref=k["q"],
            dst_ref=k["qr"].at[i],
            send_sem=s["q_s"].at[c, i],
            recv_sem=s["q_r"].at[c, i],
            device_id=(space, lax.rem(snap + 1 + i, z.n_snap)),
            device_id_type=MESH,
        )

    def ghost_copy(c, d):
        k = s["chunk"][c]
        first = z.rows + d * z.list_len
        return pltpu.make_async_remote_copy(
            src_ref=k["snd"].at[d],
            dst_ref=k["ext"].at[pl.ds(first, z.list_len)],
            send_sem=s["g_s"].at[c, d],
            recv_sem=s["g_r"].at[c, d],
            device_id=(space - OFFSETS[d], snap),
            device_id_type=MESH,
        )

    def inside(position):
        return (position >= 0) & (position < z.n_space)

    def own_modes(c):
        k = s["chunk"][c]
        for i in range(z.n_snap - 1):
            partial_copy(c, i).wait_recv()

        def block(b):
            total = k["q"][b].astype(F32)
            for i in range(z.n_snap - 1):
                total = total + k["qr"][i, b].astype(F32)
            total = total.astype(BF16)
            k["own"][b] = total
            k["ext"][b] = total
            k["st"][b, mc:, :] = total

        loop(z.rows, block)
        for d in range(z.lists):
            for t in range(z.list_len):
                k["snd"][d, t] = k["own"][ghosts[0, d, t]]

            @pl.when(inside(space - OFFSETS[d]))
            def _():
                ghost_copy(c, d).start()

            @pl.when(jnp.logical_not(inside(space + OFFSETS[d])))
            def _():
                first = z.rows + d * z.list_len
                k["ext"][first:first + z.list_len] = jnp.zeros((z.list_len, mc, bs), BF16)

    def keep(c, out, first):
        k = s["chunk"][c]
        for x, at, start, count in z.groups(c):
            @pl.when(snap == x)
            def _():
                def block(b):
                    out[at:at + count, pl.ds(pl.multiple_of(b * bs, bs), bs)] = k["st"][b, first + start:first + start + count, :]

                loop(z.rows, block)

    def apply(c):
        k = s["chunk"][c]
        for d in range(z.lists):
            @pl.when(inside(space + OFFSETS[d]))
            def _():
                ghost_copy(c, d).wait_recv()

        def row(b):
            live = counts[b]
            picked, mats = [], []
            for i in range(z.slots):
                value = k["ext"][cols[b, i]]
                picked.append(jnp.where(i < live, value, jnp.zeros_like(value)))
                mats.append(s["op"][b, i])
            result = contract_last(jnp.concatenate(picked, axis=1), jnp.concatenate(mats, axis=1))
            k["st"][b, :mc, :] = result.astype(BF16)

        loop(z.rows, row)

        def tile(t, total):
            right = jnp.concatenate([k["st"][t * TILE_BLOCKS + i] for i in range(TILE_BLOCKS)], axis=1)
            return total + contract_last(s["adj"][:, columns(t)], right)

        terms = lax.fori_loop(0, z.tiles, tile, jnp.zeros((z.modes, 2 * mc), F32))
        k["d"][...] = terms.astype(BF16).reshape(z.owners, z.piece, 2 * mc)
        for x, _, _, _ in z.groups(c):
            def send(o):
                same = (space == o) & (snap == x)

                @pl.when(same)
                def _():
                    k["rs"][me] = k["d"][o]

                @pl.when(jnp.logical_not(same))
                def _():
                    pltpu.make_async_remote_copy(
                        src_ref=k["d"].at[o],
                        dst_ref=k["rs"].at[me],
                        send_sem=s["rs_s"].at[c],
                        recv_sem=s["rs_r"].at[c],
                        device_id=(o, x),
                        device_id_type=MESH,
                    ).start()

            loop(z.owners, send)

    def settle(ref, count, sem):
        part = ref.at[pl.ds(0, count)]
        pltpu.make_async_copy(part, part, sem).wait()

    def among(c):
        found = snap == z.groups(c)[0][0]
        for x, _, _, _ in z.groups(c)[1:]:
            found = found | (snap == x)
        return found

    def add_up(c):
        k = s["chunk"][c]

        @pl.when(among(c) & (space < z.owners))
        def _():
            settle(k["rs"], z.devices - 1, s["rs_r"].at[c])
            total = lax.fori_loop(
                0,
                z.devices // 16,
                lambda i, t: t + jnp.sum(k["rs"][pl.ds(i * 16, 16)].astype(F32), axis=0),
                jnp.zeros((z.piece, 2 * mc), F32),
            )
            total = total * z.factor
            k["gs"][...] = total
            k["gat"][space] = total

            def send(i):
                pltpu.make_async_remote_copy(
                    src_ref=k["gs"],
                    dst_ref=k["gat"].at[space],
                    send_sem=s["ag_s"].at[c],
                    recv_sem=s["ag_r"].at[c],
                    device_id=(lax.rem(space + 1 + i, z.n_space), snap),
                    device_id_type=MESH,
                ).start()

            loop(z.n_space - 1, send)

    def finish(c):
        k = s["chunk"][c]
        for x, at, start, count in z.groups(c):
            @pl.when(snap == x)
            def _():
                @pl.when(space < z.owners)
                def _():
                    settle(k["gat"], z.owners - 1, s["ag_r"].at[c])

                if z.owners < z.n_space:
                    @pl.when(space >= z.owners)
                    def _():
                        settle(k["gat"], z.owners, s["ag_r"].at[c])

                whole = k["gat"][:z.owners].reshape(z.modes, 2 * mc)
                reduced_out[:, at:at + count] = whole[:, start:start + count]
                gram_out[:, at:at + count] = whole[:, mc + start:mc + start + count]

    loads[0].wait()
    s["cpt"][...] = transposed(s["cp"][...])
    loads[1].wait()
    project(0)
    pl.semaphore_wait(barrier, z.devices - 1)
    for c in range(z.chunks):
        if c:
            project(c)
        for i in range(z.n_snap - 1):
            partial_copy(c, i).start()

    loads[2].wait()
    cat = transposed(s["ca"][...])
    loads[3].wait()

    def adjoint(t):
        s["adj"][:, columns(t)] = jnp.dot(cat, s["sa"][:, columns(t)], preferred_element_type=F32).astype(BF16)

    loop(z.tiles, adjoint)
    loads[4].wait()

    last = z.chunks - 1
    for c in range(z.chunks):
        own_modes(c)
        keep(c, primal_out, mc)
        if c >= 1:
            apply(c - 1)
            keep(c - 1, applied_out, 0)
        if c >= 2:
            add_up(c - 2)
    if last >= 1:
        add_up(last - 1)
    apply(last)
    keep(last, applied_out, 0)
    add_up(last)
    for c in range(z.chunks):
        finish(c)

    for c in range(z.chunks):
        k = s["chunk"][c]
        for i in range(z.n_snap - 1):
            partial_copy(c, i).wait_send()
        for d in range(z.lists):
            @pl.when(inside(space - OFFSETS[d]))
            def _():
                ghost_copy(c, d).wait_send()

        count = len(z.groups(c)) * z.owners
        owner = among(c) & (space < z.owners)

        @pl.when(owner)
        def _():
            settle(k["rs"], count - 1, s["rs_s"].at[c])
            settle(k["gat"], z.n_space - 1, s["ag_s"].at[c])

        @pl.when(jnp.logical_not(owner))
        def _():
            settle(k["rs"], count, s["rs_s"].at[c])


def per_device(
    snaps_primal, snaps_adjoint, coef_primal, coef_adjoint, op_blocks, counts, col_index, ghost_send
):
    z = Sizes(
        lax.axis_size("space"), lax.axis_size("snap"), snaps_primal, coef_primal, op_blocks, ghost_send
    )
    any_spec = pl.BlockSpec(memory_space=pl.ANY)
    smem = pl.BlockSpec(memory_space=pltpu.SMEM)
    vmem = pl.BlockSpec(memory_space=pltpu.VMEM)
    names = scratch_of(z)
    flat, tree = jax.tree.flatten(names)

    def body(*refs):
        s = jax.tree.unflatten(tree, refs[12:])
        kernel(z, *refs[:12], s)

    flops = 2 * z.unknowns * z.modes * (2 * z.snaps + z.slots * z.bs + 2 * z.modes)
    return pl.pallas_call(
        body,
        out_shape=(
            jax.ShapeDtypeStruct((z.share, z.unknowns), BF16),
            jax.ShapeDtypeStruct((z.share, z.unknowns), BF16),
            jax.ShapeDtypeStruct((z.modes, z.share), F32),
            jax.ShapeDtypeStruct((z.modes, z.share), F32),
        ),
        in_specs=[any_spec] * 5 + [smem] * 3,
        out_specs=[vmem] * 4,
        scratch_shapes=flat,
        cost_estimate=pl.CostEstimate(flops=flops, bytes_accessed=10_000_000, transcendentals=0),
        compiler_params=pltpu.CompilerParams(
            collective_id=0, has_side_effects=True, vmem_limit_bytes=58 * 1024 * 1024
        ),
    )(snaps_primal, snaps_adjoint, coef_primal, coef_adjoint, op_blocks, counts, col_index, ghost_send)


def solution(mesh):
    placed = (
        P("snap", "space"),
        P("snap", "space"),
        P("snap", None),
        P("snap", None),
        P("space", None, None, None),
        P("space"),
        P("space", None),
        P("space", None, None),
    )
    return jax.shard_map(
        per_device,
        mesh=mesh,
        in_specs=placed,
        out_specs=(P("snap", "space"), P("snap", "space"), P(None, "snap"), P(None, "snap")),
        check_vma=False,
    )
```

time: 192 us -> 79.5 us (0.41)
  waiting for transfers between devices: 138 us -> 0 us
  Pallas kernels: 0 us -> 72.8 us
  between operations: 14 us -> 0.67 us
  starting transfers between devices: 12.7 us -> 0 us
  matrix products: 10.1 us -> 0 us
  local copies, waits for them, and re-layouts: 11.7 us -> 5.71 us
  other arithmetic: 4.07 us -> 0 us
    psum x1 -> x0, waiting for transfers between devices: 90 us -> none  [per_device(): lax.psum((products[:, :share], products[:, share:]), 'space')]
    pallas_call x0 -> x1, Pallas kernels: none -> 72.8 us  [per_device(): pl.pallas_call(body, out_shape=(jax.ShapeDtypeStruct((z.share, z.unknowns...]
    reduce_scatter x1 -> x0, waiting for transfers between devices: 42.6 us -> none  [per_device(): lax.psum_scatter(jnp.concatenate([project(coef_primal, snaps_primal), pro...]
    ppermute x4 -> x0, starting transfers between devices: 12.5 us -> none  [passed_along(): lax.ppermute(value, axis, [(source, source + steps) for source in range(f...]
    dot_general x4 -> x0, matrix products: 10.1 us -> none  [the longest x1 5.73 us: per_device(): jnp.einsum('mrkc,rkjc->mrj', picked, op_blocks, preferred_element_type=jn...]
    ppermute x4 -> x0, waiting for transfers between devices: 5.38 us -> none  [passed_along(): lax.ppermute(value, axis, [(source, source + steps) for source in range(f...]
    gather x2 -> x0, local copies, waits for them, and re-layouts: 3.63 us -> none  [the longest x1 2.94 us: per_device(): picked = jnp.take(extended, col_index, axis=1)]
    slice x2 -> x0, local copies, waits for them, and re-layouts: 3.08 us -> none  [the longest x1 2.36 us: per_device(): adjoint_share = both_shares[:, unknowns:]]
  transfers between devices with their start and end apart: 7 -> 0, of which waited for: 5 -> 0; matrix products, arithmetic and copies ran while one was open for 6% -> 0% of each run, Pallas kernels for 0% -> 0%
where the time goes in v1:
time: 79.5 us; the launch traced here: 79.1 us
  Pallas kernels  72.8 us (92%)
  local copies, waits for them, and re-layouts  5.71 us (7%)
    pallas_call x1, Pallas kernels, per_device(): pl.pallas_call(body, out_shape=(jax.ShapeDtypeStruct((z.share, z.unknowns...  72.8 us
    unnamed x11, local copies, waits for them, and re-layouts  5.71 us

profile of v1, /device:TPU:3, one launch (start us, length us, event | category | flops | bytes accessed | tf_op | source)
XLA Modules:
  0.0 79.1 jit_solution(1228148144777257890)
XLA Ops:
  0.6 1.4 %copy.12.refs_6_ = s32[24,5]{1,0:T(8,128)} copy(s32[24,5]{0,1:T(8,128)} %param.14) | data formatting | bytes 960 | tf_op args[6]
  2.0 72.8 %shard_map.111 = (bf16[128,3072]{1,0:T(8,128)(2,1)}, bf16[128,3072]{1,0:T(8,128)(2,1)}, f32[256,128]{1,0:T(8,128)}, f32[256,128]{1,0:T(8,128)}) custom-call(bf16[256,3072]{1,0:T(8,128)(2,1)} %refs_0_.1, bf16[256,3072]{1,0:T(8,128)(2,1)} %refs_1_.1, bf16[256,256]{1,0:T(8,128)(2,1)} %refs_2_.1, bf16[256,256]{1,0:T(8,128)(2,1)} %refs_3_.1, ...), custom_call_target="tpu_custom_call" | custom-call | flops 2617245696 | bytes 10000000 | tf_op jit(solution)/shard_map/pallas_call | solution.py:382
  74.8 0.0 copy-start
  74.8 0.0 copy-start.2
  74.8 0.0 copy-start.1
  74.8 2.1 %copy.17 = bf16[128,3072]{1,0:T(8,128)(2,1)} copy(bf16[128,3072]{1,0:T(8,128)(2,1)} %get-tuple-element.8) | data formatting | bytes 1572864
  76.9 0.0 copy-done
  76.9 0.9 %copy.18 = bf16[128,3072]{1,0:T(8,128)(2,1)} copy(bf16[128,3072]{1,0:T(8,128)(2,1)S(1)} %copy-done) | data formatting | bytes 1572864
  77.8 0.0 copy-done.2
  77.8 0.7 copy.19
  78.5 0.0 copy-done.1
  78.5 0.7 copy.20
Async XLA Ops:
  74.8 2.2 %copy-start = (bf16[128,3072]{1,0:T(8,128)(2,1)S(1)}, bf16[128,3072]{1,0:T(8,128)(2,1)}, u32[]{:S(2)}) copy-start(bf16[128,3072]{1,0:T(8,128)(2,1)} %get-tuple-element.9) | copy-start | bytes 2359300
  74.8 3.1 %copy-start.2 = (f32[256,128]{1,0:T(8,128)S(1)}, f32[256,128]{1,0:T(8,128)}, u32[]{:S(2)}) copy-start(f32[256,128]{1,0:T(8,128)} %get-tuple-element.10) | copy-start | bytes 393220
  74.8 3.7 %copy-start.1 = (f32[256,128]{1,0:T(8,128)S(1)}, f32[256,128]{1,0:T(8,128)}, u32[]{:S(2)}) copy-start(f32[256,128]{1,0:T(8,128)} %get-tuple-element.11) | copy-start | bytes 393220

commit v2 on v1

--- a/solution.py
+++ b/solution.py
@@ -49,7 +49,6 @@
         "own": pltpu.VMEM((b, mc, bs), BF16),
         "ext": pltpu.VMEM((b + z.lists * z.list_len, mc, bs), BF16),
         "snd": pltpu.VMEM((z.lists, z.list_len, mc, bs), BF16),
-        "st": pltpu.VMEM((b, 2 * mc, bs), BF16),
         "d": pltpu.VMEM((z.owners, z.piece, 2 * mc), BF16),
         "rs": pltpu.VMEM((z.devices, z.piece, 2 * mc), BF16),
         "gs": pltpu.VMEM((z.piece, 2 * mc), F32),
@@ -63,6 +62,12 @@
         "ca": pltpu.VMEM((z.snaps, z.modes), BF16),
         "op": pltpu.VMEM((z.rows, z.slots, bs, bs), BF16),
         "adj": pltpu.VMEM((z.modes, z.unknowns), BF16),
+        "v": pltpu.VMEM((z.tiles, z.modes, TILE_BLOCKS * z.slots * bs), BF16),
+        "po": pltpu.VMEM((z.share, z.unknowns), BF16),
+        "ao": pltpu.VMEM((z.share, z.unknowns), BF16),
+        "ro": pltpu.VMEM((z.modes, z.share), F32),
+        "go": pltpu.VMEM((z.modes, z.share), F32),
+        "store": sem((4,)),
         "cpt": pltpu.VMEM((z.modes, z.snaps), BF16),
         "load": sem((5,)),
         "q_s": sem((z.chunks, z.n_snap - 1)),
@@ -162,21 +167,36 @@
     def inside(position):
         return (position >= 0) & (position < z.n_space)
 
+    def blocks_of(t):
+        return [t * TILE_BLOCKS + i for i in range(TILE_BLOCKS)]
+
+    def carry_operator(t):
+        for i, b in enumerate(blocks_of(t)):
+            live = counts[b]
+            rows = s["adj"][:, pl.ds(pl.multiple_of(b * bs, bs), bs)]
+            mats = jnp.concatenate([s["op"][b, j] for j in range(z.slots)], axis=1)
+            part = jnp.dot(rows, mats, preferred_element_type=F32)
+            for j in range(z.slots):
+                value = part[:, j * bs:(j + 1) * bs]
+                value = jnp.where(j < live, value, jnp.zeros_like(value)).astype(BF16)
+                first = (i * z.slots + j) * bs
+                s["v"][t, :, first:first + bs] = value
+
     def own_modes(c):
         k = s["chunk"][c]
         for i in range(z.n_snap - 1):
             partial_copy(c, i).wait_recv()
 
-        def block(b):
-            total = k["q"][b].astype(F32)
-            for i in range(z.n_snap - 1):
-                total = total + k["qr"][i, b].astype(F32)
-            total = total.astype(BF16)
-            k["own"][b] = total
-            k["ext"][b] = total
-            k["st"][b, mc:, :] = total
-
-        loop(z.rows, block)
+        def tile(t):
+            for b in blocks_of(t):
+                total = k["q"][b].astype(F32)
+                for i in range(z.n_snap - 1):
+                    total = total + k["qr"][i, b].astype(F32)
+                total = total.astype(BF16)
+                k["own"][b] = total
+                k["ext"][b] = total
+
+        loop(z.tiles, tile)
         for d in range(z.lists):
             for t in range(z.list_len):
                 k["snd"][d, t] = k["own"][ghosts[0, d, t]]
@@ -190,43 +210,38 @@
                 first = z.rows + d * z.list_len
                 k["ext"][first:first + z.list_len] = jnp.zeros((z.list_len, mc, bs), BF16)
 
-    def keep(c, out, first):
-        k = s["chunk"][c]
+        def gram(t, total):
+            right = jnp.concatenate([k["own"][b] for b in blocks_of(t)], axis=1)
+            return total + contract_last(s["adj"][:, columns(t)], right)
+
+        terms = lax.fori_loop(0, z.tiles, gram, jnp.zeros((z.modes, mc), F32))
+        k["d"][:, :, mc:] = terms.astype(BF16).reshape(z.owners, z.piece, mc)
+
         for x, at, start, count in z.groups(c):
             @pl.when(snap == x)
             def _():
-                def block(b):
-                    out[at:at + count, pl.ds(pl.multiple_of(b * bs, bs), bs)] = k["st"][b, first + start:first + start + count, :]
-
-                loop(z.rows, block)
-
-    def apply(c):
+                def keep(t):
+                    for b in blocks_of(t):
+                        s["po"][at:at + count, pl.ds(pl.multiple_of(b * bs, bs), bs)] = k["own"][b, start:start + count, :]
+
+                loop(z.tiles, keep)
+
+    def terms_of(c):
         k = s["chunk"][c]
         for d in range(z.lists):
             @pl.when(inside(space + OFFSETS[d]))
             def _():
                 ghost_copy(c, d).wait_recv()
 
-        def row(b):
-            live = counts[b]
-            picked, mats = [], []
-            for i in range(z.slots):
-                value = k["ext"][cols[b, i]]
-                picked.append(jnp.where(i < live, value, jnp.zeros_like(value)))
-                mats.append(s["op"][b, i])
-            result = contract_last(jnp.concatenate(picked, axis=1), jnp.concatenate(mats, axis=1))
-            k["st"][b, :mc, :] = result.astype(BF16)
-
-        loop(z.rows, row)
-
         def tile(t, total):
-            right = jnp.concatenate([k["st"][t * TILE_BLOCKS + i] for i in range(TILE_BLOCKS)], axis=1)
-            return total + contract_last(s["adj"][:, columns(t)], right)
-
-        terms = lax.fori_loop(0, z.tiles, tile, jnp.zeros((z.modes, 2 * mc), F32))
-        k["d"][...] = terms.astype(BF16).reshape(z.owners, z.piece, 2 * mc)
+            picked = [k["ext"][cols[j, b]] for b in blocks_of(t) for j in range(z.slots)]
+            return total + contract_last(s["v"][t], jnp.concatenate(picked, axis=1))
+
+        terms = lax.fori_loop(0, z.tiles, tile, jnp.zeros((z.modes, mc), F32))
+        k["d"][:, :, :mc] = terms.astype(BF16).reshape(z.owners, z.piece, mc)
         for x, _, _, _ in z.groups(c):
-            def send(o):
+            def send(i):
+                o = lax.rem(space + 1 + i, z.owners)
                 same = (space == o) & (snap == x)
 
                 @pl.when(same)
@@ -245,6 +260,24 @@
                     ).start()
 
             loop(z.owners, send)
+
+    def apply(c, low, high):
+        k = s["chunk"][c]
+        for x, at, start, count in z.groups(c):
+            @pl.when(snap == x)
+            def _():
+                def tile(t):
+                    for b in blocks_of(low + t):
+                        live = counts[b]
+                        picked, mats = [], []
+                        for j in range(z.slots):
+                            value = k["ext"][cols[j, b]][start:start + count]
+                            picked.append(jnp.where(j < live, value, jnp.zeros_like(value)))
+                            mats.append(s["op"][b, j])
+                        result = contract_last(jnp.concatenate(picked, axis=1), jnp.concatenate(mats, axis=1))
+                        s["ao"][at:at + count, pl.ds(pl.multiple_of(b * bs, bs), bs)] = result.astype(BF16)
+
+                loop(high - low, tile)
 
     def settle(ref, count, sem):
         part = ref.at[pl.ds(0, count)]
@@ -299,8 +332,8 @@
                         settle(k["gat"], z.owners, s["ag_r"].at[c])
 
                 whole = k["gat"][:z.owners].reshape(z.modes, 2 * mc)
-                reduced_out[:, at:at + count] = whole[:, start:start + count]
-                gram_out[:, at:at + count] = whole[:, mc + start:mc + start + count]
+                s["ro"][:, at:at + count] = whole[:, start:start + count]
+                s["go"][:, at:at + count] = whole[:, mc + start:mc + start + count]
 
     loads[0].wait()
     s["cpt"][...] = transposed(s["cp"][...])
@@ -322,23 +355,36 @@
 
     loop(z.tiles, adjoint)
     loads[4].wait()
-
+    loop(z.tiles, carry_operator)
+
+    stores = [
+        pltpu.make_async_copy(s[name], target, s["store"].at[i])
+        for i, (name, target) in enumerate(
+            [("po", primal_out), ("ao", applied_out), ("ro", reduced_out), ("go", gram_out)]
+        )
+    ]
     last = z.chunks - 1
+    half = z.tiles // 2
     for c in range(z.chunks):
         own_modes(c)
-        keep(c, primal_out, mc)
+        if c == last:
+            stores[0].start()
         if c >= 1:
-            apply(c - 1)
-            keep(c - 1, applied_out, 0)
+            terms_of(c - 1)
+            apply(c - 1, 0, z.tiles)
         if c >= 2:
             add_up(c - 2)
-    if last >= 1:
+    terms_of(last)
+    if last:
         add_up(last - 1)
-    apply(last)
-    keep(last, applied_out, 0)
+    apply(last, 0, half)
     add_up(last)
+    apply(last, half, z.tiles)
+    stores[1].start()
     for c in range(z.chunks):
         finish(c)
+    stores[2].start()
+    stores[3].start()
 
     for c in range(z.chunks):
         k = s["chunk"][c]
@@ -360,6 +406,17 @@
         @pl.when(jnp.logical_not(owner))
         def _():
             settle(k["rs"], count, s["rs_s"].at[c])
+
+    for copy in stores:
+        copy.wait()
+
+
+def hand_over(*refs):
+    copies = [pltpu.make_async_copy(refs[i], refs[4 + i], refs[8].at[i]) for i in range(4)]
+    for copy in copies:
+        copy.start()
+    for copy in copies:
+        copy.wait()
 
 
 def per_device(
@@ -370,7 +427,6 @@
     )
     any_spec = pl.BlockSpec(memory_space=pl.ANY)
     smem = pl.BlockSpec(memory_space=pltpu.SMEM)
-    vmem = pl.BlockSpec(memory_space=pltpu.VMEM)
     names = scratch_of(z)
     flat, tree = jax.tree.flatten(names)
 
@@ -379,22 +435,30 @@
         kernel(z, *refs[:12], s)
 
     flops = 2 * z.unknowns * z.modes * (2 * z.snaps + z.slots * z.bs + 2 * z.modes)
-    return pl.pallas_call(
+    shapes = (
+        jax.ShapeDtypeStruct((z.share, z.unknowns), BF16),
+        jax.ShapeDtypeStruct((z.share, z.unknowns), BF16),
+        jax.ShapeDtypeStruct((z.modes, z.share), F32),
+        jax.ShapeDtypeStruct((z.modes, z.share), F32),
+    )
+    results = pl.pallas_call(
         body,
-        out_shape=(
-            jax.ShapeDtypeStruct((z.share, z.unknowns), BF16),
-            jax.ShapeDtypeStruct((z.share, z.unknowns), BF16),
-            jax.ShapeDtypeStruct((z.modes, z.share), F32),
-            jax.ShapeDtypeStruct((z.modes, z.share), F32),
-        ),
+        out_shape=shapes,
         in_specs=[any_spec] * 5 + [smem] * 3,
-        out_specs=[vmem] * 4,
+        out_specs=[any_spec] * 4,
         scratch_shapes=flat,
         cost_estimate=pl.CostEstimate(flops=flops, bytes_accessed=10_000_000, transcendentals=0),
         compiler_params=pltpu.CompilerParams(
             collective_id=0, has_side_effects=True, vmem_limit_bytes=58 * 1024 * 1024
         ),
-    )(snaps_primal, snaps_adjoint, coef_primal, coef_adjoint, op_blocks, counts, col_index, ghost_send)
+    )(snaps_primal, snaps_adjoint, coef_primal, coef_adjoint, op_blocks, counts, col_index.T, ghost_send)
+    return pl.pallas_call(
+        hand_over,
+        out_shape=shapes,
+        in_specs=[any_spec] * 4,
+        out_specs=[any_spec] * 4,
+        scratch_shapes=[pltpu.SemaphoreType.DMA((4,))],
+    )(*results)
 
 
 def solution(mesh):

time: 79.5 us -> 126 us (1.58)
  Pallas kernels: 72.8 us -> 125 us
  local copies, waits for them, and re-layouts: 5.71 us -> 0 us
    pallas_call x1 -> x2, Pallas kernels: 72.8 us -> 125 us  [the longest x1 67.9 us: per_device(): pl.pallas_call(body, out_shape=shapes, in_specs=[any_spec] * 5 + [smem] *...]
    unnamed x11 -> x0, local copies, waits for them, and re-layouts: 5.71 us -> none
where the time goes in v2:
time: 126 us; the launch traced here: 125 us
  Pallas kernels  125 us (99%)
    pallas_call x1, Pallas kernels, per_device(): pl.pallas_call(body, out_shape=shapes, in_specs=[any_spec] * 5 + [smem] *...  67.9 us
    pallas_call x1, Pallas kernels, per_device(): pl.pallas_call(hand_over, out_shape=shapes, in_specs=[any_spec] * 4, out_...  56.7 us

profile of v2, /device:TPU:3, one launch (start us, length us, event | category | flops | bytes accessed | tf_op | source)
XLA Modules:
  0.0 125.3 jit_solution(15240503059020126868)
XLA Ops:
  0.6 67.9 %shard_map.111 = (bf16[128,3072]{1,0:T(8,128)(2,1)}, bf16[128,3072]{1,0:T(8,128)(2,1)}, f32[256,128]{1,0:T(8,128)}, f32[256,128]{1,0:T(8,128)}) custom-call(bf16[256,3072]{1,0:T(8,128)(2,1)} %refs_0_.1, bf16[256,3072]{1,0:T(8,128)(2,1)} %refs_1_.1, bf16[256,256]{1,0:T(8,128)(2,1)} %refs_2_.1, bf16[256,256]{1,0:T(8,128)(2,1)} %refs_3_.1, ...), custom_call_target="tpu_custom_call" | custom-call | flops 2617245696 | bytes 10000000 | tf_op jit(solution)/shard_map/pallas_call | solution.py:444
  68.6 56.7 %shard_map.112 = (bf16[128,3072]{1,0:T(8,128)(2,1)}, bf16[128,3072]{1,0:T(8,128)(2,1)}, f32[256,128]{1,0:T(8,128)}, f32[256,128]{1,0:T(8,128)}) custom-call(bf16[128,3072]{1,0:T(8,128)(2,1)} %get-tuple-element.8.refs_0_, bf16[128,3072]{1,0:T(8,128)(2,1)} %get-tuple-element.9.refs_1_, f32[256,128]{1,0:T(8,128)} %get-tuple-element.10.refs_2_, ...), custom_call_target="tpu_custom_call" | custom-call | tf_op jit(solution)/shard_map/pallas_call | solution.py:455

commit v3 on v2

--- a/solution.py
+++ b/solution.py
@@ -12,7 +12,7 @@
 F32 = jnp.float32
 OFFSETS = (-2, -1, 1, 2)
 TILE_BLOCKS = 4
-CHUNK = 64
+CHUNKS = ((64,), (64,), (48, 48), (32,))
 
 
 class Sizes:
@@ -24,15 +24,21 @@
         self.share = self.modes // n_snap
         self.rows, self.slots, self.bs = op_blocks.shape[:3]
         self.lists, self.list_len = ghost_send.shape[1:]
-        self.mc = CHUNK
-        self.chunks = self.modes // self.mc
+        self.parts, self.sums, first = [], [], 0
+        for g, sizes in enumerate(CHUNKS):
+            self.sums.append((first, sum(sizes)))
+            for size in sizes:
+                self.parts.append((first, size, g))
+                first += size
+        assert first == self.modes
+        self.chunks = len(self.parts)
         self.piece = max(16, self.modes // n_space)
         self.owners = self.modes // self.piece
         self.tiles = self.rows // TILE_BLOCKS
         self.factor = 1.0 / math.sqrt(self.unknowns * n_space)
 
-    def groups(self, c):
-        first, last = c * self.mc, (c + 1) * self.mc
+    def groups(self, first, size):
+        last = first + size
         found = []
         for x in range(self.n_snap):
             lo, hi = max(first, x * self.share), min(last, (x + 1) * self.share)
@@ -41,19 +47,28 @@
         return found
 
 
-def scratch_of(z):
-    b, mc, bs = z.rows, z.mc, z.bs
-    one = {
+def chunk_scratch(z, mc):
+    b, bs = z.rows, z.bs
+    return {
         "q": pltpu.VMEM((b, mc, bs), BF16),
         "qr": pltpu.VMEM((z.n_snap - 1, b, mc, bs), BF16),
         "own": pltpu.VMEM((b, mc, bs), BF16),
         "ext": pltpu.VMEM((b + z.lists * z.list_len, mc, bs), BF16),
         "snd": pltpu.VMEM((z.lists, z.list_len, mc, bs), BF16),
+    }
+
+
+def sum_scratch(z, mc):
+    return {
         "d": pltpu.VMEM((z.owners, z.piece, 2 * mc), BF16),
         "rs": pltpu.VMEM((z.devices, z.piece, 2 * mc), BF16),
         "gs": pltpu.VMEM((z.piece, 2 * mc), F32),
         "gat": pltpu.VMEM((z.n_space, z.piece, 2 * mc), F32),
     }
+
+
+def scratch_of(z):
+    bs = z.bs
     sem = pltpu.SemaphoreType.DMA
     return {
         "sp": pltpu.VMEM((z.snaps, z.unknowns), BF16),
@@ -74,11 +89,12 @@
         "q_r": sem((z.chunks, z.n_snap - 1)),
         "g_s": sem((z.chunks, z.lists)),
         "g_r": sem((z.chunks, z.lists)),
-        "rs_s": sem((z.chunks,)),
-        "rs_r": sem((z.chunks,)),
-        "ag_s": sem((z.chunks,)),
-        "ag_r": sem((z.chunks,)),
-        "chunk": [dict(one) for _ in range(z.chunks)],
+        "rs_s": sem((len(z.sums),)),
+        "rs_r": sem((len(z.sums),)),
+        "ag_s": sem((len(z.sums),)),
+        "ag_r": sem((len(z.sums),)),
+        "chunk": [chunk_scratch(z, size) for _, size, _ in z.parts],
+        "sum": [sum_scratch(z, size) for _, size in z.sums],
     }
 
 
@@ -102,7 +118,7 @@
            primal_out, applied_out, reduced_out, gram_out, s):
     space, snap = lax.axis_index("space"), lax.axis_index("snap")
     me = space * z.n_snap + snap
-    bs, mc = z.bs, z.mc
+    bs = z.bs
     width = TILE_BLOCKS * bs
 
     loads = [
@@ -111,7 +127,7 @@
             [(cp_hbm, "cp"), (sp_hbm, "sp"), (ca_hbm, "ca"), (sa_hbm, "sa"), (op_hbm, "op")]
         )
     ]
-    for copy in loads:
+    for copy in loads[:2]:
         copy.start()
 
     barrier = pltpu.get_barrier_semaphore()
@@ -131,7 +147,8 @@
         return pl.ds(pl.multiple_of(t * width, width), width)
 
     def project(c):
-        coef = s["cpt"][c * mc:(c + 1) * mc, :]
+        first, mc, _ = z.parts[c]
+        coef = s["cpt"][first:first + mc, :]
         q = s["chunk"][c]["q"]
 
         def tile(t):
@@ -184,6 +201,9 @@
 
     def own_modes(c):
         k = s["chunk"][c]
+        first_mode, mc, g = z.parts[c]
+        sum_first, sum_size = z.sums[g]
+        shift = first_mode - sum_first
         for i in range(z.n_snap - 1):
             partial_copy(c, i).wait_recv()
 
@@ -215,9 +235,10 @@
             return total + contract_last(s["adj"][:, columns(t)], right)
 
         terms = lax.fori_loop(0, z.tiles, gram, jnp.zeros((z.modes, mc), F32))
-        k["d"][:, :, mc:] = terms.astype(BF16).reshape(z.owners, z.piece, mc)
-
-        for x, at, start, count in z.groups(c):
+        lane = sum_size + shift
+        s["sum"][g]["d"][:, :, lane:lane + mc] = terms.astype(BF16).reshape(z.owners, z.piece, mc)
+
+        for x, at, start, count in z.groups(first_mode, mc):
             @pl.when(snap == x)
             def _():
                 def keep(t):
@@ -228,6 +249,8 @@
 
     def terms_of(c):
         k = s["chunk"][c]
+        first_mode, mc, g = z.parts[c]
+        shift = first_mode - z.sums[g][0]
         for d in range(z.lists):
             @pl.when(inside(space + OFFSETS[d]))
             def _():
@@ -238,8 +261,11 @@
             return total + contract_last(s["v"][t], jnp.concatenate(picked, axis=1))
 
         terms = lax.fori_loop(0, z.tiles, tile, jnp.zeros((z.modes, mc), F32))
-        k["d"][:, :, :mc] = terms.astype(BF16).reshape(z.owners, z.piece, mc)
-        for x, _, _, _ in z.groups(c):
+        s["sum"][g]["d"][:, :, shift:shift + mc] = terms.astype(BF16).reshape(z.owners, z.piece, mc)
+
+    def share_out(g):
+        k = s["sum"][g]
+        for x, _, _, _ in z.groups(*z.sums[g]):
             def send(i):
                 o = lax.rem(space + 1 + i, z.owners)
                 same = (space == o) & (snap == x)
@@ -253,8 +279,8 @@
                     pltpu.make_async_remote_copy(
                         src_ref=k["d"].at[o],
                         dst_ref=k["rs"].at[me],
-                        send_sem=s["rs_s"].at[c],
-                        recv_sem=s["rs_r"].at[c],
+                        send_sem=s["rs_s"].at[g],
+                        recv_sem=s["rs_r"].at[g],
                         device_id=(o, x),
                         device_id_type=MESH,
                     ).start()
@@ -263,7 +289,7 @@
 
     def apply(c, low, high):
         k = s["chunk"][c]
-        for x, at, start, count in z.groups(c):
+        for x, at, start, count in z.groups(*z.parts[c][:2]):
             @pl.when(snap == x)
             def _():
                 def tile(t):
@@ -283,18 +309,19 @@
         part = ref.at[pl.ds(0, count)]
         pltpu.make_async_copy(part, part, sem).wait()
 
-    def among(c):
-        found = snap == z.groups(c)[0][0]
-        for x, _, _, _ in z.groups(c)[1:]:
+    def among(g):
+        found = snap == z.groups(*z.sums[g])[0][0]
+        for x, _, _, _ in z.groups(*z.sums[g])[1:]:
             found = found | (snap == x)
         return found
 
-    def add_up(c):
-        k = s["chunk"][c]
-
-        @pl.when(among(c) & (space < z.owners))
+    def add_up(g):
+        k = s["sum"][g]
+        mc = z.sums[g][1]
+
+        @pl.when(among(g) & (space < z.owners))
         def _():
-            settle(k["rs"], z.devices - 1, s["rs_r"].at[c])
+            settle(k["rs"], z.devices - 1, s["rs_r"].at[g])
             total = lax.fori_loop(
                 0,
                 z.devices // 16,
@@ -309,27 +336,28 @@
                 pltpu.make_async_remote_copy(
                     src_ref=k["gs"],
                     dst_ref=k["gat"].at[space],
-                    send_sem=s["ag_s"].at[c],
-                    recv_sem=s["ag_r"].at[c],
+                    send_sem=s["ag_s"].at[g],
+                    recv_sem=s["ag_r"].at[g],
                     device_id=(lax.rem(space + 1 + i, z.n_space), snap),
                     device_id_type=MESH,
                 ).start()
 
             loop(z.n_space - 1, send)
 
-    def finish(c):
-        k = s["chunk"][c]
-        for x, at, start, count in z.groups(c):
+    def finish(g):
+        k = s["sum"][g]
+        mc = z.sums[g][1]
+        for x, at, start, count in z.groups(*z.sums[g]):
             @pl.when(snap == x)
             def _():
                 @pl.when(space < z.owners)
                 def _():
-                    settle(k["gat"], z.owners - 1, s["ag_r"].at[c])
+                    settle(k["gat"], z.owners - 1, s["ag_r"].at[g])
 
                 if z.owners < z.n_space:
                     @pl.when(space >= z.owners)
                     def _():
-                        settle(k["gat"], z.owners, s["ag_r"].at[c])
+                        settle(k["gat"], z.owners, s["ag_r"].at[g])
 
                 whole = k["gat"][:z.owners].reshape(z.modes, 2 * mc)
                 s["ro"][:, at:at + count] = whole[:, start:start + count]
@@ -338,6 +366,8 @@
     loads[0].wait()
     s["cpt"][...] = transposed(s["cp"][...])
     loads[1].wait()
+    for copy in loads[2:]:
+        copy.start()
     project(0)
     pl.semaphore_wait(barrier, z.devices - 1)
     for c in range(z.chunks):
@@ -364,30 +394,42 @@
         )
     ]
     last = z.chunks - 1
-    half = z.tiles // 2
+
+    def ends(c):
+        return c == last or z.parts[c + 1][2] != z.parts[c][2]
+
+    def reduced_terms(c):
+        terms_of(c)
+        if ends(c):
+            share_out(z.parts[c][2])
+
+    pending = []
     for c in range(z.chunks):
         own_modes(c)
         if c == last:
             stores[0].start()
-        if c >= 1:
-            terms_of(c - 1)
-            apply(c - 1, 0, z.tiles)
-        if c >= 2:
-            add_up(c - 2)
-    terms_of(last)
-    if last:
-        add_up(last - 1)
-    apply(last, 0, half)
-    add_up(last)
-    apply(last, half, z.tiles)
+        if c:
+            reduced_terms(c - 1)
+            if c < last:
+                apply(c - 1, 0, z.tiles)
+                for g in pending:
+                    add_up(g)
+                pending = [z.parts[c - 1][2]] if ends(c - 1) else []
+            elif ends(c - 1):
+                pending.append(z.parts[c - 1][2])
+    reduced_terms(last)
+    for g in pending:
+        add_up(g)
+    apply(last - 1, 0, z.tiles)
+    add_up(z.parts[last][2])
+    apply(last, 0, z.tiles)
     stores[1].start()
-    for c in range(z.chunks):
-        finish(c)
+    for g in range(len(z.sums)):
+        finish(g)
     stores[2].start()
     stores[3].start()
 
     for c in range(z.chunks):
-        k = s["chunk"][c]
         for i in range(z.n_snap - 1):
             partial_copy(c, i).wait_send()
         for d in range(z.lists):
@@ -395,17 +437,19 @@
             def _():
                 ghost_copy(c, d).wait_send()
 
-        count = len(z.groups(c)) * z.owners
-        owner = among(c) & (space < z.owners)
+    for g in range(len(z.sums)):
+        k = s["sum"][g]
+        count = len(z.groups(*z.sums[g])) * z.owners
+        owner = among(g) & (space < z.owners)
 
         @pl.when(owner)
         def _():
-            settle(k["rs"], count - 1, s["rs_s"].at[c])
-            settle(k["gat"], z.n_space - 1, s["ag_s"].at[c])
+            settle(k["rs"], count - 1, s["rs_s"].at[g])
+            settle(k["gat"], z.n_space - 1, s["ag_s"].at[g])
 
         @pl.when(jnp.logical_not(owner))
         def _():
-            settle(k["rs"], count, s["rs_s"].at[c])
+            settle(k["rs"], count, s["rs_s"].at[g])
 
     for copy in stores:
         copy.wait()
@@ -455,7 +499,7 @@
     return pl.pallas_call(
         hand_over,
         out_shape=shapes,
-        in_specs=[any_spec] * 4,
+        in_specs=[pl.BlockSpec(memory_space=pltpu.VMEM)] * 4,
         out_specs=[any_spec] * 4,
         scratch_shapes=[pltpu.SemaphoreType.DMA((4,))],
     )(*results)

time: 126 us -> 78.8 us (0.63)
  Pallas kernels: 125 us -> 78 us
    pallas_call x1, Pallas kernels: 56.7 us -> 2.67 us  [per_device(): pl.pallas_call(hand_over, out_shape=shapes, in_specs=[pl.BlockSpec(memory...]
    pallas_call x1, Pallas kernels: 67.9 us -> 75.3 us  [per_device(): pl.pallas_call(body, out_shape=shapes, in_specs=[any_spec] * 5 + [smem] *...]
where the time goes in v3:
time: 78.8 us; the launch traced here: 78.6 us
  Pallas kernels  78 us (99%)
    pallas_call x1, Pallas kernels, per_device(): pl.pallas_call(body, out_shape=shapes, in_specs=[any_spec] * 5 + [smem] *...  75.3 us
    pallas_call x1, Pallas kernels, per_device(): pl.pallas_call(hand_over, out_shape=shapes, in_specs=[pl.BlockSpec(memory...  2.67 us

profile of v3, /device:TPU:3, one launch (start us, length us, event | category | flops | bytes accessed | tf_op | source)
XLA Modules:
  0.0 78.6 jit_solution(15327897297812307935)
XLA Ops:
  0.6 75.3 %shard_map.111 = (bf16[128,3072]{1,0:T(8,128)(2,1)}, bf16[128,3072]{1,0:T(8,128)(2,1)}, f32[256,128]{1,0:T(8,128)}, f32[256,128]{1,0:T(8,128)}) custom-call(bf16[256,3072]{1,0:T(8,128)(2,1)} %refs_0_.1, bf16[256,3072]{1,0:T(8,128)(2,1)} %refs_1_.1, bf16[256,256]{1,0:T(8,128)(2,1)} %refs_2_.1, bf16[256,256]{1,0:T(8,128)(2,1)} %refs_3_.1, ...), custom_call_target="tpu_custom_call" | custom-call | flops 2617245696 | bytes 10000000 | tf_op jit(solution)/shard_map/pallas_call | solution.py:488
  76.0 2.7 %shard_map.112 = (bf16[128,3072]{1,0:T(8,128)(2,1)}, bf16[128,3072]{1,0:T(8,128)(2,1)}, f32[256,128]{1,0:T(8,128)}, f32[256,128]{1,0:T(8,128)}) custom-call(bf16[128,3072]{1,0:T(8,128)(2,1)} %get-tuple-element.8.refs_0_, bf16[128,3072]{1,0:T(8,128)(2,1)} %get-tuple-element.9.refs_1_, f32[256,128]{1,0:T(8,128)} %get-tuple-element.10.refs_2_, ...), custom_call_target="tpu_custom_call" | custom-call | tf_op jit(solution)/shard_map/pallas_call | solution.py:499

commit v4 on v3

--- a/solution.py
+++ b/solution.py
@@ -76,8 +76,9 @@
         "cp": pltpu.VMEM((z.snaps, z.modes), BF16),
         "ca": pltpu.VMEM((z.snaps, z.modes), BF16),
         "op": pltpu.VMEM((z.rows, z.slots, bs, bs), BF16),
-        "adj": pltpu.VMEM((z.modes, z.unknowns), BF16),
-        "v": pltpu.VMEM((z.tiles, z.modes, TILE_BLOCKS * z.slots * bs), BF16),
+        "adjt": pltpu.VMEM((z.unknowns, z.modes), BF16),
+        "opt": pltpu.VMEM((z.rows, z.slots * bs, bs), BF16),
+        "vt": pltpu.VMEM((z.tiles, TILE_BLOCKS * z.slots * bs, z.modes), BF16),
         "po": pltpu.VMEM((z.share, z.unknowns), BF16),
         "ao": pltpu.VMEM((z.share, z.unknowns), BF16),
         "ro": pltpu.VMEM((z.modes, z.share), F32),
@@ -102,8 +103,8 @@
     return value.astype(F32).T.astype(BF16)
 
 
-def contract_last(a, b):
-    return lax.dot_general(a, b, (((1,), (1,)), ((), ())), preferred_element_type=F32)
+def matmul(a, b):
+    return jnp.dot(a, b, preferred_element_type=F32)
 
 
 def loop(count, body):
@@ -190,14 +191,14 @@
     def carry_operator(t):
         for i, b in enumerate(blocks_of(t)):
             live = counts[b]
-            rows = s["adj"][:, pl.ds(pl.multiple_of(b * bs, bs), bs)]
-            mats = jnp.concatenate([s["op"][b, j] for j in range(z.slots)], axis=1)
-            part = jnp.dot(rows, mats, preferred_element_type=F32)
             for j in range(z.slots):
-                value = part[:, j * bs:(j + 1) * bs]
+                s["opt"][b, j * bs:(j + 1) * bs, :] = s["op"][b, j].T
+            part = matmul(s["opt"][b], s["adjt"][pl.ds(pl.multiple_of(b * bs, bs), bs), :])
+            for j in range(z.slots):
+                value = part[j * bs:(j + 1) * bs]
                 value = jnp.where(j < live, value, jnp.zeros_like(value)).astype(BF16)
                 first = (i * z.slots + j) * bs
-                s["v"][t, :, first:first + bs] = value
+                s["vt"][t, first:first + bs, :] = value
 
     def own_modes(c):
         k = s["chunk"][c]
@@ -231,10 +232,10 @@
                 k["ext"][first:first + z.list_len] = jnp.zeros((z.list_len, mc, bs), BF16)
 
         def gram(t, total):
-            right = jnp.concatenate([k["own"][b] for b in blocks_of(t)], axis=1)
-            return total + contract_last(s["adj"][:, columns(t)], right)
-
-        terms = lax.fori_loop(0, z.tiles, gram, jnp.zeros((z.modes, mc), F32))
+            left = jnp.concatenate([k["own"][b] for b in blocks_of(t)], axis=1)
+            return total + matmul(left, s["adjt"][columns(t), :])
+
+        terms = lax.fori_loop(0, z.tiles, gram, jnp.zeros((mc, z.modes), F32)).T
         lane = sum_size + shift
         s["sum"][g]["d"][:, :, lane:lane + mc] = terms.astype(BF16).reshape(z.owners, z.piece, mc)
 
@@ -258,9 +259,9 @@
 
         def tile(t, total):
             picked = [k["ext"][cols[j, b]] for b in blocks_of(t) for j in range(z.slots)]
-            return total + contract_last(s["v"][t], jnp.concatenate(picked, axis=1))
-
-        terms = lax.fori_loop(0, z.tiles, tile, jnp.zeros((z.modes, mc), F32))
+            return total + matmul(jnp.concatenate(picked, axis=1), s["vt"][t])
+
+        terms = lax.fori_loop(0, z.tiles, tile, jnp.zeros((mc, z.modes), F32)).T
         s["sum"][g]["d"][:, :, shift:shift + mc] = terms.astype(BF16).reshape(z.owners, z.piece, mc)
 
     def share_out(g):
@@ -295,12 +296,11 @@
                 def tile(t):
                     for b in blocks_of(low + t):
                         live = counts[b]
-                        picked, mats = [], []
+                        picked = []
                         for j in range(z.slots):
                             value = k["ext"][cols[j, b]][start:start + count]
                             picked.append(jnp.where(j < live, value, jnp.zeros_like(value)))
-                            mats.append(s["op"][b, j])
-                        result = contract_last(jnp.concatenate(picked, axis=1), jnp.concatenate(mats, axis=1))
+                        result = matmul(jnp.concatenate(picked, axis=1), s["opt"][b])
                         s["ao"][at:at + count, pl.ds(pl.multiple_of(b * bs, bs), bs)] = result.astype(BF16)
 
                 loop(high - low, tile)
@@ -381,7 +381,7 @@
     loads[3].wait()
 
     def adjoint(t):
-        s["adj"][:, columns(t)] = jnp.dot(cat, s["sa"][:, columns(t)], preferred_element_type=F32).astype(BF16)
+        s["adjt"][columns(t), :] = matmul(cat, s["sa"][:, columns(t)]).T.astype(BF16)
 
     loop(z.tiles, adjoint)
     loads[4].wait()

time: 78.8 us -> 78.5 us (level)
  no operation moved by 1% of the time
where the time goes in v4:
time: 78.5 us; the launch traced here: 78.3 us
  Pallas kernels  77.6 us (99%)
    pallas_call x1, Pallas kernels, per_device(): pl.pallas_call(body, out_shape=shapes, in_specs=[any_spec] * 5 + [smem] *...  75 us
    pallas_call x1, Pallas kernels, per_device(): pl.pallas_call(hand_over, out_shape=shapes, in_specs=[pl.BlockSpec(memory...  2.67 us

profile of v4, /device:TPU:3, one launch (start us, length us, event | category | flops | bytes accessed | tf_op | source)
XLA Modules:
  0.0 78.3 jit_solution(1778991198876579251)
XLA Ops:
  0.6 75.0 %shard_map.111 = (bf16[128,3072]{1,0:T(8,128)(2,1)}, bf16[128,3072]{1,0:T(8,128)(2,1)}, f32[256,128]{1,0:T(8,128)}, f32[256,128]{1,0:T(8,128)}) custom-call(bf16[256,3072]{1,0:T(8,128)(2,1)} %refs_0_.1, bf16[256,3072]{1,0:T(8,128)(2,1)} %refs_1_.1, bf16[256,256]{1,0:T(8,128)(2,1)} %refs_2_.1, bf16[256,256]{1,0:T(8,128)(2,1)} %refs_3_.1, ...), custom_call_target="tpu_custom_call" | custom-call | flops 2617245696 | bytes 10000000 | tf_op jit(solution)/shard_map/pallas_call | solution.py:488
  75.6 2.7 %shard_map.112 = (bf16[128,3072]{1,0:T(8,128)(2,1)}, bf16[128,3072]{1,0:T(8,128)(2,1)}, f32[256,128]{1,0:T(8,128)}, f32[256,128]{1,0:T(8,128)}) custom-call(bf16[128,3072]{1,0:T(8,128)(2,1)} %get-tuple-element.8.refs_0_, bf16[128,3072]{1,0:T(8,128)(2,1)} %get-tuple-element.9.refs_1_, f32[256,128]{1,0:T(8,128)} %get-tuple-element.10.refs_2_, ...), custom_call_target="tpu_custom_call" | custom-call | tf_op jit(solution)/shard_map/pallas_call | solution.py:499

commit v5 on v4

--- a/solution.py
+++ b/solution.py
@@ -12,7 +12,7 @@
 F32 = jnp.float32
 OFFSETS = (-2, -1, 1, 2)
 TILE_BLOCKS = 4
-CHUNKS = ((64,), (64,), (48, 48), (32,))
+CHUNKS = ((64,), (64,), (64,), (32, 32))
 
 
 class Sizes:
@@ -62,8 +62,8 @@
     return {
         "d": pltpu.VMEM((z.owners, z.piece, 2 * mc), BF16),
         "rs": pltpu.VMEM((z.devices, z.piece, 2 * mc), BF16),
-        "gs": pltpu.VMEM((z.piece, 2 * mc), F32),
-        "gat": pltpu.VMEM((z.n_space, z.piece, 2 * mc), F32),
+        "gs": pltpu.VMEM((z.piece, 2 * mc), BF16),
+        "gat": pltpu.VMEM((z.n_space, z.piece, 2 * mc), BF16),
     }
 
 
@@ -86,8 +86,8 @@
         "store": sem((4,)),
         "cpt": pltpu.VMEM((z.modes, z.snaps), BF16),
         "load": sem((5,)),
-        "q_s": sem((z.chunks, z.n_snap - 1)),
-        "q_r": sem((z.chunks, z.n_snap - 1)),
+        "q_s": sem((z.chunks, z.n_snap - 1, 2)),
+        "q_r": sem((z.chunks, z.n_snap - 1, 2)),
         "g_s": sem((z.chunks, z.lists)),
         "g_r": sem((z.chunks, z.lists)),
         "rs_s": sem((len(z.sums),)),
@@ -159,13 +159,14 @@
 
         loop(z.tiles, tile)
 
-    def partial_copy(c, i):
+    def partial_copy(c, i, h):
         k = s["chunk"][c]
+        half = z.rows // 2
         return pltpu.make_async_remote_copy(
-            src_ref=k["q"],
-            dst_ref=k["qr"].at[i],
-            send_sem=s["q_s"].at[c, i],
-            recv_sem=s["q_r"].at[c, i],
+            src_ref=k["q"].at[pl.ds(h * half, half)],
+            dst_ref=k["qr"].at[i, pl.ds(h * half, half)],
+            send_sem=s["q_s"].at[c, i, h],
+            recv_sem=s["q_r"].at[c, i, h],
             device_id=(space, lax.rem(snap + 1 + i, z.n_snap)),
             device_id_type=MESH,
         )
@@ -205,8 +206,11 @@
         first_mode, mc, g = z.parts[c]
         sum_first, sum_size = z.sums[g]
         shift = first_mode - sum_first
-        for i in range(z.n_snap - 1):
-            partial_copy(c, i).wait_recv()
+        for h in range(2):
+            for i in range(z.n_snap - 1):
+                partial_copy(c, i, h).wait()
+                if c + 1 < z.chunks:
+                    partial_copy(c + 1, i, h).start()
 
         def tile(t):
             for b in blocks_of(t):
@@ -328,7 +332,7 @@
                 lambda i, t: t + jnp.sum(k["rs"][pl.ds(i * 16, 16)].astype(F32), axis=0),
                 jnp.zeros((z.piece, 2 * mc), F32),
             )
-            total = total * z.factor
+            total = (total * z.factor).astype(BF16)
             k["gs"][...] = total
             k["gat"][space] = total
 
@@ -359,7 +363,7 @@
                     def _():
                         settle(k["gat"], z.owners, s["ag_r"].at[g])
 
-                whole = k["gat"][:z.owners].reshape(z.modes, 2 * mc)
+                whole = k["gat"][:z.owners].astype(F32).reshape(z.modes, 2 * mc)
                 s["ro"][:, at:at + count] = whole[:, start:start + count]
                 s["go"][:, at:at + count] = whole[:, mc + start:mc + start + count]
 
@@ -370,11 +374,11 @@
         copy.start()
     project(0)
     pl.semaphore_wait(barrier, z.devices - 1)
-    for c in range(z.chunks):
-        if c:
-            project(c)
+    for h in range(2):
         for i in range(z.n_snap - 1):
-            partial_copy(c, i).start()
+            partial_copy(0, i, h).start()
+    for c in range(1, z.chunks):
+        project(c)
 
     loads[2].wait()
     cat = transposed(s["ca"][...])
@@ -408,15 +412,15 @@
         own_modes(c)
         if c == last:
             stores[0].start()
+        for g in pending:
+            add_up(g)
+        pending = []
         if c:
             reduced_terms(c - 1)
+            if ends(c - 1):
+                pending = [z.parts[c - 1][2]]
             if c < last:
                 apply(c - 1, 0, z.tiles)
-                for g in pending:
-                    add_up(g)
-                pending = [z.parts[c - 1][2]] if ends(c - 1) else []
-            elif ends(c - 1):
-                pending.append(z.parts[c - 1][2])
     reduced_terms(last)
     for g in pending:
         add_up(g)
@@ -430,8 +434,6 @@
     stores[3].start()
 
     for c in range(z.chunks):
-        for i in range(z.n_snap - 1):
-            partial_copy(c, i).wait_send()
         for d in range(z.lists):
             @pl.when(inside(space - OFFSETS[d]))
             def _():

time: 78.5 us -> 71.4 us (0.910)
  Pallas kernels: 77.6 us -> 70.6 us
    pallas_call x1, Pallas kernels: 75 us -> 67.9 us  [per_device(): pl.pallas_call(body, out_shape=shapes, in_specs=[any_spec] * 5 + [smem] *...]
where the time goes in v5:
time: 71.4 us; the launch traced here: 71.2 us
  Pallas kernels  70.6 us (99%)
    pallas_call x1, Pallas kernels, per_device(): pl.pallas_call(body, out_shape=shapes, in_specs=[any_spec] * 5 + [smem] *...  67.9 us
    pallas_call x1, Pallas kernels, per_device(): pl.pallas_call(hand_over, out_shape=shapes, in_specs=[pl.BlockSpec(memory...  2.67 us

profile of v5, /device:TPU:3, one launch (start us, length us, event | category | flops | bytes accessed | tf_op | source)
XLA Modules:
  0.0 71.2 jit_solution(2502017549013078209)
XLA Ops:
  0.6 67.9 %shard_map.111 = (bf16[128,3072]{1,0:T(8,128)(2,1)}, bf16[128,3072]{1,0:T(8,128)(2,1)}, f32[256,128]{1,0:T(8,128)}, f32[256,128]{1,0:T(8,128)}) custom-call(bf16[256,3072]{1,0:T(8,128)(2,1)} %refs_0_.1, bf16[256,3072]{1,0:T(8,128)(2,1)} %refs_1_.1, bf16[256,256]{1,0:T(8,128)(2,1)} %refs_2_.1, bf16[256,256]{1,0:T(8,128)(2,1)} %refs_3_.1, ...), custom_call_target="tpu_custom_call" | custom-call | flops 2617245696 | bytes 10000000 | tf_op jit(solution)/shard_map/pallas_call | solution.py:490
  68.5 2.7 %shard_map.112 = (bf16[128,3072]{1,0:T(8,128)(2,1)}, bf16[128,3072]{1,0:T(8,128)(2,1)}, f32[256,128]{1,0:T(8,128)}, f32[256,128]{1,0:T(8,128)}) custom-call(bf16[128,3072]{1,0:T(8,128)(2,1)} %get-tuple-element.8.refs_0_, bf16[128,3072]{1,0:T(8,128)(2,1)} %get-tuple-element.9.refs_1_, f32[256,128]{1,0:T(8,128)} %get-tuple-element.10.refs_2_, ...), custom_call_target="tpu_custom_call" | custom-call | tf_op jit(solution)/shard_map/pallas_call | solution.py:501

commit v6 on v5

--- a/solution.py
+++ b/solution.py
@@ -58,10 +58,12 @@
     }
 
 
-def sum_scratch(z, mc):
+def sum_scratch(z, mc, near):
     return {
+        "pt": pltpu.VMEM((z.piece, 2 * mc), F32),
+        "ps": pltpu.VMEM((z.n_snap - 1, z.piece, 2 * mc), F32),
         "d": pltpu.VMEM((z.owners, z.piece, 2 * mc), BF16),
-        "rs": pltpu.VMEM((z.devices, z.piece, 2 * mc), BF16),
+        "rs": pltpu.VMEM((z.n_space if near else z.devices, z.piece, 2 * mc), BF16),
         "gs": pltpu.VMEM((z.piece, 2 * mc), BF16),
         "gat": pltpu.VMEM((z.n_space, z.piece, 2 * mc), BF16),
     }
@@ -92,10 +94,12 @@
         "g_r": sem((z.chunks, z.lists)),
         "rs_s": sem((len(z.sums),)),
         "rs_r": sem((len(z.sums),)),
+        "ps_s": sem((len(z.sums),)),
+        "ps_r": sem((len(z.sums),)),
         "ag_s": sem((len(z.sums),)),
         "ag_r": sem((len(z.sums),)),
         "chunk": [chunk_scratch(z, size) for _, size, _ in z.parts],
-        "sum": [sum_scratch(z, size) for _, size in z.sums],
+        "sum": [sum_scratch(z, size, g + 1 < len(z.sums)) for g, (_, size) in enumerate(z.sums)],
     }
 
 
@@ -268,22 +272,59 @@
         terms = lax.fori_loop(0, z.tiles, tile, jnp.zeros((mc, z.modes), F32)).T
         s["sum"][g]["d"][:, :, shift:shift + mc] = terms.astype(BF16).reshape(z.owners, z.piece, mc)
 
+    def is_near(g):
+        return g + 1 < len(z.sums)
+
+    def targets(g):
+        return [x for x, _, _, _ in z.groups(*z.sums[g])]
+
+    def sum_of(g):
+        k = s["sum"][g]
+        slots = z.n_space if is_near(g) else z.devices
+        settle(k["rs"], slots - 1, s["rs_r"].at[g])
+        return lax.fori_loop(
+            0,
+            slots // 16,
+            lambda i, t: t + jnp.sum(k["rs"][pl.ds(i * 16, 16)].astype(F32), axis=0),
+            jnp.zeros((z.piece, 2 * z.sums[g][1]), F32),
+        )
+
+    def send_on(g):
+        k = s["sum"][g]
+
+        @pl.when(space < z.owners)
+        def _():
+            k["pt"][...] = sum_of(g)
+            for x in targets(g):
+                @pl.when(snap != x)
+                def _():
+                    pltpu.make_async_remote_copy(
+                        src_ref=k["pt"],
+                        dst_ref=k["ps"].at[lax.rem(snap - x + z.n_snap, z.n_snap) - 1],
+                        send_sem=s["ps_s"].at[g],
+                        recv_sem=s["ps_r"].at[g],
+                        device_id=(space, x),
+                        device_id_type=MESH,
+                    ).start()
+
     def share_out(g):
         k = s["sum"][g]
-        for x, _, _, _ in z.groups(*z.sums[g]):
+        near = is_near(g)
+        for x in [snap] if near else targets(g):
             def send(i):
                 o = lax.rem(space + 1 + i, z.owners)
+                slot = space if near else me
                 same = (space == o) & (snap == x)
 
                 @pl.when(same)
                 def _():
-                    k["rs"][me] = k["d"][o]
+                    k["rs"][slot] = k["d"][o]
 
                 @pl.when(jnp.logical_not(same))
                 def _():
                     pltpu.make_async_remote_copy(
                         src_ref=k["d"].at[o],
-                        dst_ref=k["rs"].at[me],
+                        dst_ref=k["rs"].at[slot],
                         send_sem=s["rs_s"].at[g],
                         recv_sem=s["rs_r"].at[g],
                         device_id=(o, x),
@@ -325,13 +366,13 @@
 
         @pl.when(among(g) & (space < z.owners))
         def _():
-            settle(k["rs"], z.devices - 1, s["rs_r"].at[g])
-            total = lax.fori_loop(
-                0,
-                z.devices // 16,
-                lambda i, t: t + jnp.sum(k["rs"][pl.ds(i * 16, 16)].astype(F32), axis=0),
-                jnp.zeros((z.piece, 2 * mc), F32),
-            )
+            if is_near(g):
+                total = k["pt"][...]
+                settle(k["ps"], z.n_snap - 1, s["ps_r"].at[g])
+                for i in range(z.n_snap - 1):
+                    total = total + k["ps"][i]
+            else:
+                total = sum_of(g)
             total = (total * z.factor).astype(BF16)
             k["gs"][...] = total
             k["gat"][space] = total
@@ -407,14 +448,16 @@
         if ends(c):
             share_out(z.parts[c][2])
 
-    pending = []
+    pending, passed = [], []
     for c in range(z.chunks):
         own_modes(c)
         if c == last:
             stores[0].start()
+        for g in passed:
+            add_up(g)
         for g in pending:
-            add_up(g)
-        pending = []
+            send_on(g)
+        passed, pending = pending, []
         if c:
             reduced_terms(c - 1)
             if ends(c - 1):
@@ -422,7 +465,7 @@
             if c < last:
                 apply(c - 1, 0, z.tiles)
     reduced_terms(last)
-    for g in pending:
+    for g in passed:
         add_up(g)
     apply(last - 1, 0, z.tiles)
     add_up(z.parts[last][2])
@@ -441,17 +484,40 @@
 
     for g in range(len(z.sums)):
         k = s["sum"][g]
-        count = len(z.groups(*z.sums[g])) * z.owners
-        owner = among(g) & (space < z.owners)
-
-        @pl.when(owner)
+        found = targets(g)
+        owner = space < z.owners
+        if is_near(g):
+            @pl.when(owner)
+            def _():
+                settle(k["rs"], z.owners - 1, s["rs_s"].at[g])
+
+                @pl.when(among(g))
+                def _():
+                    if len(found) > 1:
+                        settle(k["ps"], len(found) - 1, s["ps_s"].at[g])
+
+                @pl.when(jnp.logical_not(among(g)))
+                def _():
+                    settle(k["ps"], len(found), s["ps_s"].at[g])
+
+            if z.owners < z.n_space:
+                @pl.when(jnp.logical_not(owner))
+                def _():
+                    settle(k["rs"], z.owners, s["rs_s"].at[g])
+        else:
+            count = len(found) * z.owners
+
+            @pl.when(owner & among(g))
+            def _():
+                settle(k["rs"], count - 1, s["rs_s"].at[g])
+
+            @pl.when(jnp.logical_not(owner & among(g)))
+            def _():
+                settle(k["rs"], count, s["rs_s"].at[g])
+
+        @pl.when(owner & among(g))
         def _():
-            settle(k["rs"], count - 1, s["rs_s"].at[g])
             settle(k["gat"], z.n_space - 1, s["ag_s"].at[g])
-
-        @pl.when(jnp.logical_not(owner))
-        def _():
-            settle(k["rs"], count, s["rs_s"].at[g])
 
     for copy in stores:
         copy.wait()

time: 71.4 us -> 69.5 us (0.973)
  Pallas kernels: 70.6 us -> 68.7 us
    pallas_call x1, Pallas kernels: 67.9 us -> 66 us  [per_device(): pl.pallas_call(body, out_shape=shapes, in_specs=[any_spec] * 5 + [smem] *...]
where the time goes in v6:
time: 69.5 us; the launch traced here: 69.3 us
  Pallas kernels  68.7 us (99%)
    pallas_call x1, Pallas kernels, per_device(): pl.pallas_call(body, out_shape=shapes, in_specs=[any_spec] * 5 + [smem] *...  66 us
    pallas_call x1, Pallas kernels, per_device(): pl.pallas_call(hand_over, out_shape=shapes, in_specs=[pl.BlockSpec(memory...  2.67 us

profile of v6, /device:TPU:3, one launch (start us, length us, event | category | flops | bytes accessed | tf_op | source)
XLA Modules:
  0.0 69.3 jit_solution(5328659229263401196)
XLA Ops:
  0.6 66.0 %shard_map.111 = (bf16[128,3072]{1,0:T(8,128)(2,1)}, bf16[128,3072]{1,0:T(8,128)(2,1)}, f32[256,128]{1,0:T(8,128)}, f32[256,128]{1,0:T(8,128)}) custom-call(bf16[256,3072]{1,0:T(8,128)(2,1)} %refs_0_.1, bf16[256,3072]{1,0:T(8,128)(2,1)} %refs_1_.1, bf16[256,256]{1,0:T(8,128)(2,1)} %refs_2_.1, bf16[256,256]{1,0:T(8,128)(2,1)} %refs_3_.1, ...), custom_call_target="tpu_custom_call" | custom-call | flops 2617245696 | bytes 10000000 | tf_op jit(solution)/shard_map/pallas_call | solution.py:556
  66.6 2.7 %shard_map.112 = (bf16[128,3072]{1,0:T(8,128)(2,1)}, bf16[128,3072]{1,0:T(8,128)(2,1)}, f32[256,128]{1,0:T(8,128)}, f32[256,128]{1,0:T(8,128)}) custom-call(bf16[128,3072]{1,0:T(8,128)(2,1)} %get-tuple-element.8.refs_0_, bf16[128,3072]{1,0:T(8,128)(2,1)} %get-tuple-element.9.refs_1_, f32[256,128]{1,0:T(8,128)} %get-tuple-element.10.refs_2_, ...), custom_call_target="tpu_custom_call" | custom-call | tf_op jit(solution)/shard_map/pallas_call | solution.py:567

commit v7 on v6

--- a/solution.py
+++ b/solution.py
@@ -213,8 +213,8 @@
         for h in range(2):
             for i in range(z.n_snap - 1):
                 partial_copy(c, i, h).wait()
-                if c + 1 < z.chunks:
-                    partial_copy(c + 1, i, h).start()
+                if c + 1 + h < z.chunks:
+                    partial_copy(c + 1 + h, i, 1 - h).start()
 
         def tile(t):
             for b in blocks_of(t):
@@ -420,6 +420,9 @@
             partial_copy(0, i, h).start()
     for c in range(1, z.chunks):
         project(c)
+        if c == 1:
+            for i in range(z.n_snap - 1):
+                partial_copy(1, i, 0).start()
 
     loads[2].wait()
     cat = transposed(s["ca"][...])

time: 69.5 us -> 68.9 us (level)
  no operation moved by 1% of the time
where the time goes in v7:
time: 68.9 us; the launch traced here: 68.7 us
  Pallas kernels  68.1 us (99%)
    pallas_call x1, Pallas kernels, per_device(): pl.pallas_call(body, out_shape=shapes, in_specs=[any_spec] * 5 + [smem] *...  65.4 us
    pallas_call x1, Pallas kernels, per_device(): pl.pallas_call(hand_over, out_shape=shapes, in_specs=[pl.BlockSpec(memory...  2.67 us

profile of v7, /device:TPU:3, one launch (start us, length us, event | category | flops | bytes accessed | tf_op | source)
XLA Modules:
  0.0 68.7 jit_solution(16784371962461663643)
XLA Ops:
  0.6 65.4 %shard_map.111 = (bf16[128,3072]{1,0:T(8,128)(2,1)}, bf16[128,3072]{1,0:T(8,128)(2,1)}, f32[256,128]{1,0:T(8,128)}, f32[256,128]{1,0:T(8,128)}) custom-call(bf16[256,3072]{1,0:T(8,128)(2,1)} %refs_0_.1, bf16[256,3072]{1,0:T(8,128)(2,1)} %refs_1_.1, bf16[256,256]{1,0:T(8,128)(2,1)} %refs_2_.1, bf16[256,256]{1,0:T(8,128)(2,1)} %refs_3_.1, ...), custom_call_target="tpu_custom_call" | custom-call | flops 2617245696 | bytes 10000000 | tf_op jit(solution)/shard_map/pallas_call | solution.py:559
  66.0 2.7 %shard_map.112 = (bf16[128,3072]{1,0:T(8,128)(2,1)}, bf16[128,3072]{1,0:T(8,128)(2,1)}, f32[256,128]{1,0:T(8,128)}, f32[256,128]{1,0:T(8,128)}) custom-call(bf16[128,3072]{1,0:T(8,128)(2,1)} %get-tuple-element.8.refs_0_, bf16[128,3072]{1,0:T(8,128)(2,1)} %get-tuple-element.9.refs_1_, f32[256,128]{1,0:T(8,128)} %get-tuple-element.10.refs_2_, ...), custom_call_target="tpu_custom_call" | custom-call | tf_op jit(solution)/shard_map/pallas_call | solution.py:570
